TPU v7x, 32 devices: a whole 2x2x4 slice. The times are simulated.
32 devices in a mesh: seq: 4 (over y, x), kvh: 2 (over core), rep: 4 (over z).
Axes of the slice: x: 2, y: 2, z: 4, core: 2. Of those that a mesh axis runs over, the one named last changes fastest.
Arguments:
- queries: bfloat16 [32, 2, 4, 128], P('rep', 'kvh'), parts along dimension 0, may hold values from -6 to 6
- slot_key_cache: bfloat16 [32, 2, 1024, 128], P('rep', 'kvh', 'seq'), parts along dimension 0, may hold values from -6 to 6
- slot_value_cache: bfloat16 [32, 2, 1024, 128], P('rep', 'kvh', 'seq'), parts along dimension 0, may hold values from -24 to 24
- lengths: int32 [32], P('rep'), parts along dimension 0, may hold values from 128 to 1024, as said below
- output_weight_matrix: bfloat16 [2, 4, 128, 8192], P('kvh', 'seq'), may hold values from -0.25 to 0.25
- residual: float32 [32, 8192], P('rep', ('seq', 'kvh')), parts along dimension 0, may hold values from -6 to 6
Outputs:
- hidden_out: float32 [32, 8192], P('rep', ('seq', 'kvh')), parts along dimension 0
There are 4 independent parts, one for each index of `rep`. A program takes and returns all parts, laid end to end along the dimension named above; an argument that names none is the same for every part. Nothing has to cross between parts.
Inputs may be any that keep to these rules, and one draw needn't show every extreme that they name: Some row has 1024 live positions and some row 128; a row's live block count is lengths rounded up to whole blocks of 32.
All inputs are finite; a program needn't handle non-finite values.
Results may differ from a plain program's by a relative error of at most 0.0028.
Values sent between devices are 32-bit elements; how exact they have to be, the bound alone decides.
A program may use at most 64 MiB of HBM per device.

v0:
```python
import math

import jax
import jax.numpy as jnp
from jax import lax
from jax.sharding import PartitionSpec as P

BLOCK_POSITIONS = 32


def combined_all(value, axis, combine):
    everything = jax.tree.map(lambda part: lax.all_gather(part, axis), value)
    first = jax.tree.map(lambda part: part[0], everything)

    def step(k, so_far):
        return combine(so_far, jax.tree.map(lambda part: part[k], everything))

    return lax.fori_loop(1, lax.axis_size(axis), step, first)


def join_partials(first, second):
    first_out, first_log = first
    second_out, second_log = second
    highest = jnp.maximum(first_log, second_log)
    first_factor = jnp.exp(first_log - highest)
    second_factor = jnp.exp(second_log - highest)
    denominator = first_factor + second_factor
    joined = (
        first_factor[..., None] * first_out + second_factor[..., None] * second_out
    ) / denominator[..., None]
    return (joined, highest + jnp.log(denominator))


def body(queries, slot_key_cache, slot_value_cache, lengths, output_weight_matrix, residual):
    shard_count = lax.axis_size("seq")
    shard_index = lax.axis_index("seq")
    group_query = queries[:, 0]
    key_rows = slot_key_cache[:, 0]
    value_rows = slot_value_cache[:, 0]
    slot_count = key_rows.shape[1]
    head_size = key_rows.shape[2]
    scale = 1.0 / math.sqrt(head_size)
    slot_ids = jnp.arange(slot_count, dtype=jnp.int32)
    positions = (
        slot_ids // BLOCK_POSITIONS * shard_count + shard_index
    ) * BLOCK_POSITIONS + slot_ids % BLOCK_POSITIONS
    visible = positions[None, :] < lengths[:, None]
    scores = (
        jnp.einsum("bgd,bcd->gbc", group_query, key_rows, preferred_element_type=jnp.float32)
        * scale
    )
    scores = jnp.where(visible[None], scores, -1e30)
    maximum = jnp.max(scores, axis=2)
    weights = jnp.exp(scores - maximum[..., None])
    totals = jnp.sum(weights, axis=2)
    rounded = weights.astype(jnp.bfloat16)
    summed = jnp.einsum("gbc,bcd->gbd", rounded, value_rows, preferred_element_type=jnp.float32)
    partial_value = summed / totals[..., None]
    log_sums = maximum + jnp.log(totals)
    joined, joined_log = combined_all((partial_value, log_sums), "seq", join_partials)
    attention_output = lax.dynamic_slice_in_dim(joined, shard_index, 1, 0)[0]
    out_rows = output_weight_matrix[0, 0]
    contrib = jnp.dot(
        attention_output.astype(jnp.bfloat16), out_rows, preferred_element_type=jnp.float32
    )
    reduced = lax.psum_scatter(contrib, ("seq", "kvh"), scatter_dimension=1, tiled=True)
    return residual + reduced


def solution(mesh):
    in_specs = (
        P("rep", "kvh", None, None),
        P("rep", "kvh", "seq", None),
        P("rep", "kvh", "seq", None),
        P("rep"),
        P("kvh", "seq", None, None),
        P("rep", ("seq", "kvh")),
    )
    out_specs = P("rep", ("seq", "kvh"))
    return jax.shard_map(body, mesh=mesh, in_specs=in_specs, out_specs=out_specs, check_vma=False)
```

profile of v0, /device:TPU:0, one launch (start us, length us, event | category | flops | bytes accessed | tf_op | source)
XLA Modules:
  0.0 71.9 jit_solution(5219733012140657298)
XLA Ops:
  6.5 0.0 copy-start
  6.5 0.0 reduce-scatter.2.cloned.1.call-start
  6.5 0.9 %broadcast_compare_fusion = pred[8,256]{1,0:T(8,128)(4,1)S(1)} fusion(s32[256]{0:T(256)S(1)} %fusion.19, s32[8]{0:T(128)} %param.11), kind=kLoop, calls=%fused_computation.24 | loop fusion | flops 2048 | bytes 3104 | tf_op jit(solution)/shard_map/lt | solution.py:47
  7.4 1.4 %fusion.25 = (f32[4,8]{0,1:T(8,128)S(1)}, f32[4,8,256]{2,0,1:T(4,128)S(1)}) fusion(bf16[8,1,4,128]{3,2,1,0:T(4,128)(2,1)} %param.8, bf16[8,1,256,128]{3,2,1,0:T(8,128)(2,1)} %param.9, pred[8,256]{1,0:T(8,128)(4,1)S(1)} %broadcast_compare_fusion), kind=kOutput, calls=%fused_computation.39 | convolution fusion | flops 2121696 | bytes 567424 | tf_op jit(solution)/shard_map/bgd,bcd->gbc/dot_general | solution.py:49
  8.8 0.0 copy-start.1
  8.8 0.2 fusion.10
  9.0 1.3 %fusion.7 = f32[4,8,128]{2,0,1:T(4,128)S(1)} fusion(bf16[8,1,256,128]{3,2,1,0:T(8,128)(2,1)} %param.10, f32[4,8,256]{2,0,1:T(4,128)S(1)} %get-tuple-element.158, f32[4,8]{0,1:T(8,128)S(1)} %get-tuple-element.157, f32[4,8]{0,1:T(8,128)S(1)} %fusion.10), kind=kOutput, calls=%fused_computation.14 | convolution fusion | flops 2117632 | bytes 573696 | tf_op jit(solution)/shard_map/gbc,bcd->gbd/dot_general | solution.py:57
  10.3 0.1 copy.12
  10.3 9.5 %all-gather.2 = f32[4,4,8]{2,1,0:T(4,128)S(1)} all-gather(f32[1,4,8]{2,1,0:T(4,128)S(1)} %bitcast.53), channel_id=3, replica_groups=mesh['seq'=4,'kvh'=2,'rep'=4] {'seq'}, dimensions={0}, use_global_device_ids=true | all-gather | bytes 640 | tf_op jit(solution)/shard_map/all_gather | solution.py:12
  19.9 8.2 %all-gather = f32[16,8,128]{2,1,0:T(8,128)S(1)} all-gather(f32[4,8,128]{2,1,0:T(8,128)S(1)} %copy.11), channel_id=2, replica_groups=mesh['seq'=4,'kvh'=2,'rep'=4] {'seq'}, dimensions={0}, use_global_device_ids=true | all-gather | bytes 81920 | tf_op jit(solution)/shard_map/all_gather | solution.py:12
  28.1 0.4 while.17
  28.1 0.1 fusion.27
  28.3 0.1 fusion.27
  28.4 0.1 fusion.27
  28.5 0.0 copy-done
  28.5 1.1 %fusion.3 = f32[8,8192]{1,0:T(8,128)} fusion(bf16[1,1,128,8192]{3,2,1,0:T(8,128)(2,1)S(1)} %copy-done, f32[4,8,128]{2,1,0:T(8,128)S(1)} %get-tuple-element.137, s32[]{:T(128)S(6)} %select_n.45), kind=kOutput, calls=%fused_computation.8 | convolution fusion | flops 16777216 | bytes 2361348 | tf_op jit(solution)/shard_map/dot_general | solution.py:63
  29.6 0.0 reduce-scatter.2.cloned.1.call-update
  29.6 34.0 %reduce-scatter.2.cloned.1.call-done = f32[8,1024]{1,0:T(8,128)} async-done(((f32[8,8192]{1,0:T(8,128)}), f32[8,1024]{1,0:T(8,128)}) %reduce-scatter.2.cloned.1.call-update) | async-done | bytes 32784 | tf_op jit(solution)/shard_map/reduce_scatter | solution.py:66
  63.6 0.0 copy-done.1
  63.6 1.4 %add.124 = f32[8,1024]{1,0:T(8,128)} add(f32[8,1024]{1,0:T(8,128)S(1)} %copy-done.1, f32[8,1024]{1,0:T(8,128)} %reduce-scatter.2.cloned.1.call-done) | non-fusion elementwise | flops 8192 | bytes 98304 | tf_op jit(solution)/shard_map/add | solution.py:67
  (8 shorter events, 0.1 us)
Async XLA Ops:
  6.5 22.0 %copy-start = (bf16[1,1,128,8192]{3,2,1,0:T(8,128)(2,1)S(1)}, bf16[1,1,128,8192]{3,2,1,0:T(8,128)(2,1)}, u32[]{:S(2)}) copy-start(bf16[1,1,128,8192]{3,2,1,0:T(8,128)(2,1)} %param.12) | copy-start | bytes 6291460
  6.5 57.1 %reduce-scatter.2.cloned.1.call-start = ((), (), s32[]{:S(2)}) async-start(), calls=%async_computation.1 | async-start | bytes 294912 | tf_op jit(solution)/shard_map/reduce_scatter | solution.py:66
  8.8 54.9 %copy-start.1 = (f32[8,1024]{1,0:T(8,128)S(1)}, f32[8,1024]{1,0:T(8,128)}, u32[]{:S(2)}) copy-start(f32[8,1024]{1,0:T(8,128)} %param.13) | copy-start | bytes 98308
Sparse Core Ops, SparseCore 0:
  29.7 33.8 reduce-scatter.1
where the time goes:
time: 72.1 us; the launch traced here: 71.9 us
  waiting for transfers between devices  34 us (47%)
  blocking collectives  17.7 us (25%)
  between operations  13.4 us (19%)
  matrix products  3.72 us (5%)
  other arithmetic  2.78 us (4%)
    reduce_scatter x1, waiting for transfers between devices, body(): lax.psum_scatter(contrib, ('seq', 'kvh'), scatter_dimension=1, tiled=True)  34 us
    all_gather x2, blocking collectives, combined_all(): everything = jax.tree.map(lambda part: lax.all_gather(part, axis), value)  17.7 us
  transfers between devices with their start and end apart: 1, of which 1 were waited for; matrix products, arithmetic and copies ran while one was open for 0% of the time, Pallas kernels for 0%

commit v1 on v0

v1 whole, which is shorter than its diff:
```python
import functools
import math

import jax
import jax.numpy as jnp
from jax import lax
from jax.experimental import pallas as pl
from jax.experimental.pallas import tpu as pltpu
from jax.sharding import PartitionSpec as P

BLOCK_POSITIONS = 32
MESH = pl.DeviceIdType.MESH


def partner(me, step, count):
    result = 0
    bit = 1
    while bit < count:
        own = lax.rem(lax.div(me, bit), 2)
        result = result + bit * (1 - own if (step // bit) % 2 else own)
        bit *= 2
    return result


def kernel(
    n_seq, n_kvh,
    lengths, queries, keys, values, weights, residual, out,
    q_buf, q_rows, k_buf, v_buf, w_buf, r_buf,
    part_send, part_recv, core_send, core_recv, seq_send, seq_recv, contrib,
    load_sem, ps_sem, pr_sem, cs_sem, cr_sem, ss_sem, sr_sem,
):
    seq = lax.axis_index("seq")
    kvh = lax.axis_index("kvh")
    rows, _, heads, size = queries.shape
    slots = keys.shape[2]
    share = out.shape[1]
    blocks = n_seq * n_kvh

    loads = [
        pltpu.make_async_copy(queries, q_buf, load_sem.at[0]),
        pltpu.make_async_copy(keys, k_buf, load_sem.at[1]),
        pltpu.make_async_copy(values, v_buf, load_sem.at[2]),
        pltpu.make_async_copy(weights.at[0, 0], w_buf, load_sem.at[3]),
        pltpu.make_async_copy(residual, r_buf, load_sem.at[4]),
    ]
    for load in loads:
        load.start()

    seq_peers = [partner(seq, i, n_seq) for i in range(n_seq)]
    kvh_peers = [partner(kvh, j, n_kvh) for j in range(n_kvh)]
    barrier = pltpu.get_barrier_semaphore()
    for i in range(1, n_seq):
        pl.semaphore_signal(barrier, inc=1, device_id={"seq": seq_peers[i]}, device_id_type=MESH)
    for j in range(1, n_kvh):
        pl.semaphore_signal(barrier, inc=1, device_id={"kvh": kvh_peers[j]}, device_id_type=MESH)

    row = lax.broadcasted_iota(jnp.int32, (rows, slots), 0)
    slot = lax.broadcasted_iota(jnp.int32, (rows, slots), 1)
    length = jnp.zeros((rows, slots), jnp.int32)
    for b in range(rows):
        length = jnp.where(row == b, lengths[b], length)
    position = (slot // BLOCK_POSITIONS * n_seq + seq) * BLOCK_POSITIONS + slot % BLOCK_POSITIONS
    live = position < length
    out_row = lax.broadcasted_iota(jnp.int32, (rows, size), 0)

    loads[0].wait()
    for b in range(rows):
        q_rows[pl.ds(b * heads, heads), :] = q_buf[b, 0].astype(jnp.float32)
    q = jnp.concatenate(
        [q_rows[pl.ds(g, rows, stride=heads), :] for g in range(heads)], axis=0
    ).astype(jnp.bfloat16)

    loads[1].wait()
    scores = jnp.zeros((heads, rows, slots), jnp.float32)
    for b in range(rows):
        full = lax.dot_general(
            q, k_buf[b, 0], (((1,), (1,)), ((), ())), preferred_element_type=jnp.float32
        ).reshape(heads, rows, slots)
        scores = jnp.where((row == b)[None], full, scores)
    scores = jnp.where(live[None], scores * (1.0 / math.sqrt(size)), -1e30)
    top = jnp.max(scores, axis=2, keepdims=True)
    probs = jnp.exp(scores - top)
    total = jnp.sum(probs, axis=2, keepdims=True)
    probs = probs.reshape(heads * rows, slots).astype(jnp.bfloat16)
    loads[2].wait()
    summed = jnp.zeros((heads, rows, size), jnp.float32)
    for b in range(rows):
        full = jnp.dot(probs, v_buf[b, 0], preferred_element_type=jnp.float32)
        summed = jnp.where((out_row == b)[None], full.reshape(heads, rows, size), summed)
    part_send[:, :rows, :] = summed / total
    part_send[:, rows:, :] = jnp.broadcast_to(top + jnp.log(total), (heads, rows, size))

    pl.semaphore_wait(barrier, n_seq - 1 + n_kvh - 1)
    sends = []
    order = list(range(n_seq - 1, 0, -1))
    part_copies = {}
    for i in order:
        copy = pltpu.make_async_remote_copy(
            src_ref=part_send.at[seq_peers[i]],
            dst_ref=part_recv.at[i],
            send_sem=ps_sem.at[i],
            recv_sem=pr_sem.at[i],
            device_id={"seq": seq_peers[i]},
            device_id_type=MESH,
        )
        copy.start()
        part_copies[i] = copy
        sends.append(copy)

    loads[3].wait()
    loads[4].wait()
    parts = [part_send[seq]]
    for i in range(1, n_seq):
        part_copies[i].wait_recv()
        parts.append(part_recv[i])
    highest = functools.reduce(jnp.maximum, [part[rows:] for part in parts])
    factors = [jnp.exp(part[rows:] - highest) for part in parts]
    joined = sum(factor * part[:rows] for factor, part in zip(factors, parts))
    attended = (joined / sum(factors)).astype(jnp.bfloat16)

    aligned = share % 128 == 0
    if not aligned:
        for first in range(0, blocks * share, 1024):
            tile = jnp.dot(
                attended, w_buf[:, first:first + 1024], preferred_element_type=jnp.float32
            )
            for block in range(1024 // share):
                contrib[first // share + block] = tile[:, block * share:(block + 1) * share]

    def contribution(i, j):
        block = seq_peers[i] * n_kvh + kvh_peers[j]
        if not aligned:
            return contrib[block]
        columns = pl.ds(pl.multiple_of(block * share, share), share)
        return jnp.dot(attended, w_buf[:, columns], preferred_element_type=jnp.float32)

    order.append(0)
    core_copies = {}
    for i in order:
        for j in range(1, n_kvh):
            core_send[i, j] = contribution(i, j)
            copy = pltpu.make_async_remote_copy(
                src_ref=core_send.at[i, j],
                dst_ref=core_recv.at[i, j],
                send_sem=cs_sem.at[i, j],
                recv_sem=cr_sem.at[i, j],
                device_id={"kvh": kvh_peers[j]},
                device_id_type=MESH,
            )
            copy.start()
            core_copies[i, j] = copy
            sends.append(copy)
    seq_copies = {}
    for i in order:
        own = contribution(i, 0)
        for j in range(1, n_kvh):
            core_copies[i, j].wait_recv()
            own = own + core_recv[i, j]
        if i:
            seq_send[i] = own
            copy = pltpu.make_async_remote_copy(
                src_ref=seq_send.at[i],
                dst_ref=seq_recv.at[i],
                send_sem=ss_sem.at[i],
                recv_sem=sr_sem.at[i],
                device_id={"seq": seq_peers[i]},
                device_id_type=MESH,
            )
            copy.start()
            seq_copies[i] = copy
            sends.append(copy)
        else:
            result = r_buf[...] + own
    for i in order[:-1][::-1]:
        seq_copies[i].wait_recv()
        result = result + seq_recv[i]
    out[...] = result
    for copy in sends:
        copy.wait_send()


def body(n_seq, n_kvh, queries, keys, values, lengths, weights, residual):
    rows, _, heads, size = queries.shape
    slots = keys.shape[2]
    features = weights.shape[3]
    share = residual.shape[1]
    f32, bf16 = jnp.float32, jnp.bfloat16
    dma = pltpu.SemaphoreType.DMA
    in_hbm = pl.BlockSpec(memory_space=pltpu.HBM)
    return pl.pallas_call(
        functools.partial(kernel, n_seq, n_kvh),
        out_shape=jax.ShapeDtypeStruct((rows, share), f32),
        in_specs=[pl.BlockSpec(memory_space=pltpu.SMEM)] + [in_hbm] * 5,
        out_specs=pl.BlockSpec(memory_space=pltpu.VMEM),
        scratch_shapes=[
            pltpu.VMEM((rows, 1, heads, size), bf16),
            pltpu.VMEM((rows * heads, size), f32),
            pltpu.VMEM((rows, 1, slots, size), bf16),
            pltpu.VMEM((rows, 1, slots, size), bf16),
            pltpu.VMEM((size, features), bf16),
            pltpu.VMEM((rows, share), f32),
            pltpu.VMEM((heads, 2 * rows, size), f32),
            pltpu.VMEM((n_seq, 2 * rows, size), f32),
            pltpu.VMEM((n_seq, n_kvh, rows, share), f32),
            pltpu.VMEM((n_seq, n_kvh, rows, share), f32),
            pltpu.VMEM((n_seq, rows, share), f32),
            pltpu.VMEM((n_seq, rows, share), f32),
            pltpu.VMEM((n_seq * n_kvh if share % 128 else 1, rows, share), f32),
            dma((5,)),
            dma((n_seq,)),
            dma((n_seq,)),
            dma((n_seq, n_kvh)),
            dma((n_seq, n_kvh)),
            dma((n_seq,)),
            dma((n_seq,)),
        ],
        compiler_params=pltpu.CompilerParams(
            collective_id=0, has_side_effects=True, vmem_limit_bytes=40 * 1024 * 1024
        ),
        cost_estimate=pl.CostEstimate(
            flops=2 * rows * size * features, bytes_accessed=2 * size * features, transcendentals=0
        ),
    )(lengths, queries, keys, values, weights, residual)


def solution(mesh):
    in_specs = (
        P("rep", "kvh", None, None),
        P("rep", "kvh", "seq", None),
        P("rep", "kvh", "seq", None),
        P("rep"),
        P("kvh", "seq", None, None),
        P("rep", ("seq", "kvh")),
    )
    out_specs = P("rep", ("seq", "kvh"))
    run = functools.partial(body, mesh.shape["seq"], mesh.shape["kvh"])
    return jax.shard_map(run, mesh=mesh, in_specs=in_specs, out_specs=out_specs, check_vma=False)
```

time: 72.1 us -> 19.4 us (0.27)
  waiting for transfers between devices: 34 us -> 0 us
  blocking collectives: 17.7 us -> 0 us
  between operations: 13.4 us -> 0.02 us
  Pallas kernels: 0 us -> 12.6 us
  local copies, waits for them, and re-layouts: 0.09 us -> 6.4 us
  matrix products: 3.72 us -> 0 us
  other arithmetic: 2.78 us -> 0 us
    reduce_scatter x1 -> x0, waiting for transfers between devices: 34 us -> none  [body(): lax.psum_scatter(contrib, ('seq', 'kvh'), scatter_dimension=1, tiled=True)]
    all_gather x2 -> x0, blocking collectives: 17.7 us -> none  [combined_all(): everything = jax.tree.map(lambda part: lax.all_gather(part, axis), value)]
    pallas_call x0 -> x1, Pallas kernels: none -> 12.6 us  [body(): pl.pallas_call(functools.partial(kernel, n_seq, n_kvh), out_shape=jax.Sha...]
    unnamed x4 -> x13, local copies, waits for them, and re-layouts: 0.01 us -> 6.4 us
    dot_general x3 -> x0, matrix products: 3.72 us -> none  [the longest x1 1.36 us: body(): jnp.einsum('bgd,bcd->gbc', group_query, key_rows, preferred_element_type=...]
    add x6 -> x0, other arithmetic: 1.47 us -> none  [the longest x1 1.38 us: body(): return residual + reduced]
    lt x1 -> x0, other arithmetic: 0.88 us -> none  [body(): visible = positions[None, :] < lengths[:, None]]
  transfers between devices with their start and end apart: 1 -> 0, of which waited for: 1 -> 0; matrix products, arithmetic and copies ran while one was open for 0% -> 0% of each run, Pallas kernels for 0% -> 0%
where the time goes in v1:
time: 19.4 us; the launch traced here: 19.1 us
  Pallas kernels  12.6 us (65%)
  local copies, waits for them, and re-layouts  6.4 us (33%)
    pallas_call x1, Pallas kernels, body(): pl.pallas_call(functools.partial(kernel, n_seq, n_kvh), out_shape=jax.Sha...  12.6 us
    unnamed x13, local copies, waits for them, and re-layouts  6.4 us

profile of v1, /device:TPU:0, one launch (start us, length us, event | category | flops | bytes accessed | tf_op | source)
XLA Modules:
  0.0 19.1 jit_solution(579814194914132611)
XLA Ops:
  0.0 0.0 copy-start
  0.0 1.6 %copy-done = bf16[1,1,128,8192]{3,2,1,0:T(8,128)(2,1)S(1)} copy-done((bf16[1,1,128,8192]{3,2,1,0:T(8,128)(2,1)S(1)}, bf16[1,1,128,8192]{3,2,1,0:T(8,128)(2,1)}, u32[]{:S(2)}) %copy-start) | copy-done | bytes 2097176
  1.6 0.0 copy-start.1
  1.6 1.0 %copy-done.1 = bf16[8,1,256,128]{3,2,1,0:T(8,128)(2,1)S(1)} copy-done((bf16[8,1,256,128]{3,2,1,0:T(8,128)(2,1)S(1)}, bf16[8,1,256,128]{3,2,1,0:T(8,128)(2,1)}, u32[]{:S(2)}) %copy-start.1) | copy-done | bytes 524312
  2.6 0.0 copy-start.2
  2.6 1.0 %copy-done.2 = bf16[8,1,256,128]{3,2,1,0:T(8,128)(2,1)S(1)} copy-done((bf16[8,1,256,128]{3,2,1,0:T(8,128)(2,1)S(1)}, bf16[8,1,256,128]{3,2,1,0:T(8,128)(2,1)}, u32[]{:S(2)}) %copy-start.2) | copy-done | bytes 524312
  3.7 0.0 copy-start.3
  3.7 0.8 %copy-done.3 = f32[8,1024]{1,0:T(8,128)S(1)} copy-done((f32[8,1024]{1,0:T(8,128)S(1)}, f32[8,1024]{1,0:T(8,128)}, u32[]{:S(2)}) %copy-start.3) | copy-done | bytes 32792
  4.4 0.0 copy-start.4
  4.4 0.7 %copy-done.4 = bf16[8,1,4,128]{3,2,1,0:T(4,128)(2,1)S(1)} copy-done((bf16[8,1,4,128]{3,2,1,0:T(4,128)(2,1)S(1)}, bf16[8,1,4,128]{3,2,1,0:T(4,128)(2,1)}, u32[]{:S(2)}) %copy-start.4) | copy-done | bytes 8216
  5.1 0.0 copy-start.5
  5.1 0.7 %copy-done.5 = s32[8]{0:T(128)S(1)} copy-done((s32[8]{0:T(128)S(1)}, s32[8]{0:T(128)}, u32[]{:S(2)}) %copy-start.5) | copy-done | bytes 56
  5.8 12.6 %shard_map.64 = f32[8,1024]{1,0:T(8,128)S(1)} custom-call(s32[8]{0:T(128)S(1)} %copy-done.5, bf16[8,1,4,128]{3,2,1,0:T(4,128)(2,1)S(1)} %copy-done.4, bf16[8,1,256,128]{3,2,1,0:T(8,128)(2,1)S(1)} %copy-done.1, bf16[8,1,256,128]{3,2,1,0:T(8,128)(2,1)S(1)} %copy-done.2, bf16[1,1,128,8192]{3,2,1,0:T(8,128)(2,1)S(1)} %copy-done, f32[8,1024]{1,0:T(8,128)S(1)} %copy-done.3), custom_call_target="tpu_custom_call" | custom-call | flops 16777216 | bytes 2097152 | tf_op jit(solution)/shard_map/pallas_call | solution.py:190
  18.4 0.6 %copy.8 = f32[8,1024]{1,0:T(8,128)} copy(f32[8,1024]{1,0:T(8,128)S(1)} %shard_map.64) | data formatting | bytes 65536
Async XLA Ops:
  0.0 1.6 %copy-start = (bf16[1,1,128,8192]{3,2,1,0:T(8,128)(2,1)S(1)}, bf16[1,1,128,8192]{3,2,1,0:T(8,128)(2,1)}, u32[]{:S(2)}) copy-start(bf16[1,1,128,8192]{3,2,1,0:T(8,128)(2,1)} %weights.1) | copy-start | bytes 6291460
  1.6 1.0 %copy-start.1 = (bf16[8,1,256,128]{3,2,1,0:T(8,128)(2,1)S(1)}, bf16[8,1,256,128]{3,2,1,0:T(8,128)(2,1)}, u32[]{:S(2)}) copy-start(bf16[8,1,256,128]{3,2,1,0:T(8,128)(2,1)} %keys.1) | copy-start | bytes 1572868
  2.6 1.0 %copy-start.2 = (bf16[8,1,256,128]{3,2,1,0:T(8,128)(2,1)S(1)}, bf16[8,1,256,128]{3,2,1,0:T(8,128)(2,1)}, u32[]{:S(2)}) copy-start(bf16[8,1,256,128]{3,2,1,0:T(8,128)(2,1)} %values.1) | copy-start | bytes 1572868
  3.7 0.8 %copy-start.3 = (f32[8,1024]{1,0:T(8,128)S(1)}, f32[8,1024]{1,0:T(8,128)}, u32[]{:S(2)}) copy-start(f32[8,1024]{1,0:T(8,128)} %residual.1) | copy-start | bytes 98308
  4.4 0.7 %copy-start.4 = (bf16[8,1,4,128]{3,2,1,0:T(4,128)(2,1)S(1)}, bf16[8,1,4,128]{3,2,1,0:T(4,128)(2,1)}, u32[]{:S(2)}) copy-start(bf16[8,1,4,128]{3,2,1,0:T(4,128)(2,1)} %queries.1) | copy-start | bytes 24580
  5.1 0.7 %copy-start.5 = (s32[8]{0:T(128)S(1)}, s32[8]{0:T(128)}, u32[]{:S(2)}) copy-start(s32[8]{0:T(128)} %lengths.1) | copy-start | bytes 100

commit v2 on v1

--- a/solution.py
+++ b/solution.py
@@ -25,7 +25,7 @@
 def kernel(
     n_seq, n_kvh,
     lengths, queries, keys, values, weights, residual, out,
-    q_buf, q_rows, k_buf, v_buf, w_buf, r_buf,
+    l_buf, q_buf, q_rows, k_buf, v_buf, w_buf, r_buf,
     part_send, part_recv, core_send, core_recv, seq_send, seq_recv, contrib,
     load_sem, ps_sem, pr_sem, cs_sem, cr_sem, ss_sem, sr_sem,
 ):
@@ -42,9 +42,10 @@
         pltpu.make_async_copy(values, v_buf, load_sem.at[2]),
         pltpu.make_async_copy(weights.at[0, 0], w_buf, load_sem.at[3]),
         pltpu.make_async_copy(residual, r_buf, load_sem.at[4]),
+        pltpu.make_async_copy(lengths, l_buf, load_sem.at[5]),
     ]
-    for load in loads:
-        load.start()
+    for n in (5, 0, 1, 2, 3, 4):
+        loads[n].start()
 
     seq_peers = [partner(seq, i, n_seq) for i in range(n_seq)]
     kvh_peers = [partner(kvh, j, n_kvh) for j in range(n_kvh)]
@@ -57,8 +58,9 @@
     row = lax.broadcasted_iota(jnp.int32, (rows, slots), 0)
     slot = lax.broadcasted_iota(jnp.int32, (rows, slots), 1)
     length = jnp.zeros((rows, slots), jnp.int32)
-    for b in range(rows):
-        length = jnp.where(row == b, lengths[b], length)
+    loads[5].wait()
+    for b in range(rows):
+        length = jnp.where(row == b, l_buf[b], length)
     position = (slot // BLOCK_POSITIONS * n_seq + seq) * BLOCK_POSITIONS + slot % BLOCK_POSITIONS
     live = position < length
     out_row = lax.broadcasted_iota(jnp.int32, (rows, size), 0)
@@ -151,8 +153,11 @@
             core_copies[i, j] = copy
             sends.append(copy)
     seq_copies = {}
-    for i in order:
-        own = contribution(i, 0)
+    seq_send[order[0]] = contribution(order[0], 0)
+    for i, after in zip(order, order[1:] + [None]):
+        if after is not None:
+            seq_send[after] = contribution(after, 0)
+        own = seq_send[i]
         for j in range(1, n_kvh):
             core_copies[i, j].wait_recv()
             own = own + core_recv[i, j]
@@ -190,9 +195,10 @@
     return pl.pallas_call(
         functools.partial(kernel, n_seq, n_kvh),
         out_shape=jax.ShapeDtypeStruct((rows, share), f32),
-        in_specs=[pl.BlockSpec(memory_space=pltpu.SMEM)] + [in_hbm] * 5,
+        in_specs=[in_hbm] * 6,
         out_specs=pl.BlockSpec(memory_space=pltpu.VMEM),
         scratch_shapes=[
+            pltpu.SMEM((rows,), jnp.int32),
             pltpu.VMEM((rows, 1, heads, size), bf16),
             pltpu.VMEM((rows * heads, size), f32),
             pltpu.VMEM((rows, 1, slots, size), bf16),
@@ -206,7 +212,7 @@
             pltpu.VMEM((n_seq, rows, share), f32),
             pltpu.VMEM((n_seq, rows, share), f32),
             pltpu.VMEM((n_seq * n_kvh if share % 128 else 1, rows, share), f32),
-            dma((5,)),
+            dma((6,)),
             dma((n_seq,)),
             dma((n_seq,)),
             dma((n_seq, n_kvh)),
@@ -220,7 +226,10 @@
         cost_estimate=pl.CostEstimate(
             flops=2 * rows * size * features, bytes_accessed=2 * size * features, transcendentals=0
         ),
-    )(lengths, queries, keys, values, weights, residual)
+    )(*[
+        pltpu.with_memory_space_constraint(array, pltpu.HBM)
+        for array in (lengths, queries, keys, values, weights, residual)
+    ])
 
 
 def solution(mesh):

time: 19.4 us -> 12.8 us (0.66)
  local copies, waits for them, and re-layouts: 6.4 us -> 0.62 us
  Pallas kernels: 12.6 us -> 12 us
    unnamed x13 -> x1, local copies, waits for them, and re-layouts: 6.4 us -> 0.62 us
    pallas_call x1, Pallas kernels: 12.6 us -> 12 us  [body(): pl.pallas_call(functools.partial(kernel, n_seq, n_kvh), out_shape=jax.Sha...]
where the time goes in v2:
time: 12.8 us; the launch traced here: 12.6 us
  Pallas kernels  12 us (94%)
  local copies, waits for them, and re-layouts  0.62 us (5%)
    pallas_call x1, Pallas kernels, body(): pl.pallas_call(functools.partial(kernel, n_seq, n_kvh), out_shape=jax.Sha...  12 us
    unnamed x1, local copies, waits for them, and re-layouts  0.62 us

profile of v2, /device:TPU:0, one launch (start us, length us, event | category | flops | bytes accessed | tf_op | source)
XLA Modules:
  0.0 12.6 jit_solution(9203107268439867719)
XLA Ops:
  0.0 12.0 %shard_map.64 = f32[8,1024]{1,0:T(8,128)S(1)} custom-call(s32[8]{0:T(128)} %lengths.1, bf16[8,1,4,128]{3,2,1,0:T(4,128)(2,1)} %queries.1, bf16[8,1,256,128]{3,2,1,0:T(8,128)(2,1)} %keys.1, bf16[8,1,256,128]{3,2,1,0:T(8,128)(2,1)} %values.1, bf16[1,1,128,8192]{3,2,1,0:T(8,128)(2,1)} %weights.1, f32[8,1024]{1,0:T(8,128)} %residual.1), custom_call_target="tpu_custom_call" | custom-call | flops 16777216 | bytes 2097152 | tf_op jit(solution)/shard_map/pallas_call | solution.py:195
  12.0 0.6 %copy.8 = f32[8,1024]{1,0:T(8,128)} copy(f32[8,1024]{1,0:T(8,128)S(1)} %shard_map.64) | data formatting | bytes 65536

commit v3 on v2

--- a/solution.py
+++ b/solution.py
@@ -9,6 +9,7 @@
 from jax.sharding import PartitionSpec as P
 
 BLOCK_POSITIONS = 32
+DIRECT_COLUMNS = 256
 MESH = pl.DeviceIdType.MESH
 
 
@@ -23,11 +24,12 @@
 
 
 def kernel(
-    n_seq, n_kvh,
+    n_seq, n_kvh, cut,
     lengths, queries, keys, values, weights, residual, out,
     l_buf, q_buf, q_rows, k_buf, v_buf, w_buf, r_buf,
-    part_send, part_recv, core_send, core_recv, seq_send, seq_recv, contrib,
-    load_sem, ps_sem, pr_sem, cs_sem, cr_sem, ss_sem, sr_sem,
+    part_send, part_recv, direct_send, direct_recv, core_send, core_recv,
+    seq_send, seq_recv, contrib,
+    load_sem, ps_sem, pr_sem, ds_sem, dr_sem, cs_sem, cr_sem, ss_sem, sr_sem,
 ):
     seq = lax.axis_index("seq")
     kvh = lax.axis_index("kvh")
@@ -36,45 +38,58 @@
     share = out.shape[1]
     blocks = n_seq * n_kvh
 
-    loads = [
-        pltpu.make_async_copy(queries, q_buf, load_sem.at[0]),
-        pltpu.make_async_copy(keys, k_buf, load_sem.at[1]),
-        pltpu.make_async_copy(values, v_buf, load_sem.at[2]),
-        pltpu.make_async_copy(weights.at[0, 0], w_buf, load_sem.at[3]),
-        pltpu.make_async_copy(residual, r_buf, load_sem.at[4]),
-        pltpu.make_async_copy(lengths, l_buf, load_sem.at[5]),
-    ]
-    for n in (5, 0, 1, 2, 3, 4):
-        loads[n].start()
+    step = rows // 4
+    loads = {
+        "lengths": pltpu.make_async_copy(lengths, l_buf, load_sem.at[0]),
+        "queries": pltpu.make_async_copy(queries, q_buf, load_sem.at[1]),
+    }
+    for n in range(4):
+        some = pl.ds(n * step, step)
+        loads["keys", n * step] = pltpu.make_async_copy(
+            keys.at[some], k_buf.at[some], load_sem.at[2 + n]
+        )
+    for n in range(4):
+        some = pl.ds(n * step, step)
+        loads["values", n * step] = pltpu.make_async_copy(
+            values.at[some], v_buf.at[some], load_sem.at[6 + n]
+        )
+    loads["weights"] = pltpu.make_async_copy(weights.at[0, 0], w_buf, load_sem.at[10])
+    loads["residual"] = pltpu.make_async_copy(residual, r_buf, load_sem.at[11])
+    for load in loads.values():
+        load.start()
 
     seq_peers = [partner(seq, i, n_seq) for i in range(n_seq)]
     kvh_peers = [partner(kvh, j, n_kvh) for j in range(n_kvh)]
     barrier = pltpu.get_barrier_semaphore()
-    for i in range(1, n_seq):
-        pl.semaphore_signal(barrier, inc=1, device_id={"seq": seq_peers[i]}, device_id_type=MESH)
-    for j in range(1, n_kvh):
-        pl.semaphore_signal(barrier, inc=1, device_id={"kvh": kvh_peers[j]}, device_id_type=MESH)
+    greeted = 0
+    for i in range(n_seq):
+        for j in range(n_kvh):
+            if (i or j) and (cut or not (i and j)):
+                target = {"seq": seq_peers[i], "kvh": kvh_peers[j]}
+                pl.semaphore_signal(barrier, inc=1, device_id=target, device_id_type=MESH)
+                greeted += 1
 
     row = lax.broadcasted_iota(jnp.int32, (rows, slots), 0)
     slot = lax.broadcasted_iota(jnp.int32, (rows, slots), 1)
     length = jnp.zeros((rows, slots), jnp.int32)
-    loads[5].wait()
+    loads["lengths"].wait()
     for b in range(rows):
         length = jnp.where(row == b, l_buf[b], length)
     position = (slot // BLOCK_POSITIONS * n_seq + seq) * BLOCK_POSITIONS + slot % BLOCK_POSITIONS
     live = position < length
     out_row = lax.broadcasted_iota(jnp.int32, (rows, size), 0)
 
-    loads[0].wait()
+    loads["queries"].wait()
     for b in range(rows):
         q_rows[pl.ds(b * heads, heads), :] = q_buf[b, 0].astype(jnp.float32)
     q = jnp.concatenate(
         [q_rows[pl.ds(g, rows, stride=heads), :] for g in range(heads)], axis=0
     ).astype(jnp.bfloat16)
 
-    loads[1].wait()
     scores = jnp.zeros((heads, rows, slots), jnp.float32)
     for b in range(rows):
+        if b % step == 0:
+            loads["keys", b].wait()
         full = lax.dot_general(
             q, k_buf[b, 0], (((1,), (1,)), ((), ())), preferred_element_type=jnp.float32
         ).reshape(heads, rows, slots)
@@ -84,15 +99,16 @@
     probs = jnp.exp(scores - top)
     total = jnp.sum(probs, axis=2, keepdims=True)
     probs = probs.reshape(heads * rows, slots).astype(jnp.bfloat16)
-    loads[2].wait()
     summed = jnp.zeros((heads, rows, size), jnp.float32)
     for b in range(rows):
+        if b % step == 0:
+            loads["values", b].wait()
         full = jnp.dot(probs, v_buf[b, 0], preferred_element_type=jnp.float32)
         summed = jnp.where((out_row == b)[None], full.reshape(heads, rows, size), summed)
     part_send[:, :rows, :] = summed / total
     part_send[:, rows:, :] = jnp.broadcast_to(top + jnp.log(total), (heads, rows, size))
 
-    pl.semaphore_wait(barrier, n_seq - 1 + n_kvh - 1)
+    pl.semaphore_wait(barrier, greeted)
     sends = []
     order = list(range(n_seq - 1, 0, -1))
     part_copies = {}
@@ -109,8 +125,8 @@
         part_copies[i] = copy
         sends.append(copy)
 
-    loads[3].wait()
-    loads[4].wait()
+    loads["weights"].wait()
+    loads["residual"].wait()
     parts = [part_send[seq]]
     for i in range(1, n_seq):
         part_copies[i].wait_recv()
@@ -129,43 +145,66 @@
             for block in range(1024 // share):
                 contrib[first // share + block] = tile[:, block * share:(block + 1) * share]
 
-    def contribution(i, j):
+    def contribution(i, j, first, count):
         block = seq_peers[i] * n_kvh + kvh_peers[j]
         if not aligned:
             return contrib[block]
-        columns = pl.ds(pl.multiple_of(block * share, share), share)
+        columns = pl.ds(pl.multiple_of(block * share + first, 128), count)
         return jnp.dot(attended, w_buf[:, columns], preferred_element_type=jnp.float32)
 
     order.append(0)
+    low, high = pl.ds(0, cut), pl.ds(cut, share - cut)
+    direct_copies = {}
     core_copies = {}
     for i in order:
+        for j in range(n_kvh):
+            if i and cut:
+                direct_send[i, j] = contribution(i, j, 0, cut)
+                target = {"seq": seq_peers[i]}
+                if j:
+                    target["kvh"] = kvh_peers[j]
+                copy = pltpu.make_async_remote_copy(
+                    src_ref=direct_send.at[i, j],
+                    dst_ref=direct_recv.at[i, j],
+                    send_sem=ds_sem.at[i, j],
+                    recv_sem=dr_sem.at[i, j],
+                    device_id=target,
+                    device_id_type=MESH,
+                )
+                copy.start()
+                direct_copies[i, j] = copy
+                sends.append(copy)
         for j in range(1, n_kvh):
-            core_send[i, j] = contribution(i, j)
+            first = cut if i else 0
+            if first < share:
+                part = pl.ds(first, share - first)
+                core_send[i, j, :, part] = contribution(i, j, first, share - first)
+                copy = pltpu.make_async_remote_copy(
+                    src_ref=core_send.at[i, j, :, part],
+                    dst_ref=core_recv.at[i, j, :, part],
+                    send_sem=cs_sem.at[i, j],
+                    recv_sem=cr_sem.at[i, j],
+                    device_id={"kvh": kvh_peers[j]},
+                    device_id_type=MESH,
+                )
+                copy.start()
+                core_copies[i, j] = copy
+                sends.append(copy)
+    seq_copies = {}
+    if cut < share:
+        waiting = order[:-1]
+        seq_send[waiting[0], :, high] = contribution(waiting[0], 0, cut, share - cut)
+        for i, after in zip(waiting, waiting[1:] + [None]):
+            if after is not None:
+                seq_send[after, :, high] = contribution(after, 0, cut, share - cut)
+            own = seq_send[i, :, high]
+            for j in range(1, n_kvh):
+                core_copies[i, j].wait_recv()
+                own = own + core_recv[i, j, :, high]
+            seq_send[i, :, high] = own
             copy = pltpu.make_async_remote_copy(
-                src_ref=core_send.at[i, j],
-                dst_ref=core_recv.at[i, j],
-                send_sem=cs_sem.at[i, j],
-                recv_sem=cr_sem.at[i, j],
-                device_id={"kvh": kvh_peers[j]},
-                device_id_type=MESH,
-            )
-            copy.start()
-            core_copies[i, j] = copy
-            sends.append(copy)
-    seq_copies = {}
-    seq_send[order[0]] = contribution(order[0], 0)
-    for i, after in zip(order, order[1:] + [None]):
-        if after is not None:
-            seq_send[after] = contribution(after, 0)
-        own = seq_send[i]
-        for j in range(1, n_kvh):
-            core_copies[i, j].wait_recv()
-            own = own + core_recv[i, j]
-        if i:
-            seq_send[i] = own
-            copy = pltpu.make_async_remote_copy(
-                src_ref=seq_send.at[i],
-                dst_ref=seq_recv.at[i],
+                src_ref=seq_send.at[i, :, high],
+                dst_ref=seq_recv.at[i, :, high],
                 send_sem=ss_sem.at[i],
                 recv_sem=sr_sem.at[i],
                 device_id={"seq": seq_peers[i]},
@@ -174,12 +213,24 @@
             copy.start()
             seq_copies[i] = copy
             sends.append(copy)
-        else:
-            result = r_buf[...] + own
-    for i in order[:-1][::-1]:
-        seq_copies[i].wait_recv()
-        result = result + seq_recv[i]
+    result = r_buf[...] + contribution(0, 0, 0, share)
+    for j in range(1, n_kvh):
+        core_copies[0, j].wait_recv()
+        result = result + core_recv[0, j]
     out[...] = result
+    if cut:
+        result = out[:, low]
+        for i in order[:-1][::-1]:
+            for j in range(n_kvh):
+                direct_copies[i, j].wait_recv()
+                result = result + direct_recv[i, j]
+        out[:, low] = result
+    if cut < share:
+        result = out[:, high]
+        for i in order[:-1][::-1]:
+            seq_copies[i].wait_recv()
+            result = result + seq_recv[i, :, high]
+        out[:, high] = result
     for copy in sends:
         copy.wait_send()
 
@@ -189,11 +240,12 @@
     slots = keys.shape[2]
     features = weights.shape[3]
     share = residual.shape[1]
+    cut = min(DIRECT_COLUMNS, share) if share % 128 == 0 else 0
     f32, bf16 = jnp.float32, jnp.bfloat16
     dma = pltpu.SemaphoreType.DMA
     in_hbm = pl.BlockSpec(memory_space=pltpu.HBM)
     return pl.pallas_call(
-        functools.partial(kernel, n_seq, n_kvh),
+        functools.partial(kernel, n_seq, n_kvh, cut),
         out_shape=jax.ShapeDtypeStruct((rows, share), f32),
         in_specs=[in_hbm] * 6,
         out_specs=pl.BlockSpec(memory_space=pltpu.VMEM),
@@ -207,14 +259,18 @@
             pltpu.VMEM((rows, share), f32),
             pltpu.VMEM((heads, 2 * rows, size), f32),
             pltpu.VMEM((n_seq, 2 * rows, size), f32),
+            pltpu.VMEM((n_seq, n_kvh, rows, max(cut, 128)), f32),
+            pltpu.VMEM((n_seq, n_kvh, rows, max(cut, 128)), f32),
             pltpu.VMEM((n_seq, n_kvh, rows, share), f32),
             pltpu.VMEM((n_seq, n_kvh, rows, share), f32),
             pltpu.VMEM((n_seq, rows, share), f32),
             pltpu.VMEM((n_seq, rows, share), f32),
             pltpu.VMEM((n_seq * n_kvh if share % 128 else 1, rows, share), f32),
-            dma((6,)),
+            dma((12,)),
             dma((n_seq,)),
             dma((n_seq,)),
+            dma((n_seq, n_kvh)),
+            dma((n_seq, n_kvh)),
             dma((n_seq, n_kvh)),
             dma((n_seq, n_kvh)),
             dma((n_seq,)),

time: 12.8 us -> 13.7 us (1.070)
  Pallas kernels: 12 us -> 12.9 us
    pallas_call x1, Pallas kernels: 12 us -> 12.9 us  [body(): pl.pallas_call(functools.partial(kernel, n_seq, n_kvh, cut), out_shape=ja...]
where the time goes in v3:
time: 13.7 us; the launch traced here: 13.5 us
  Pallas kernels  12.9 us (94%)
  local copies, waits for them, and re-layouts  0.62 us (5%)
    pallas_call x1, Pallas kernels, body(): pl.pallas_call(functools.partial(kernel, n_seq, n_kvh, cut), out_shape=ja...  12.9 us
    unnamed x1, local copies, waits for them, and re-layouts  0.62 us

profile of v3, /device:TPU:0, one launch (start us, length us, event | category | flops | bytes accessed | tf_op | source)
XLA Modules:
  0.0 13.5 jit_solution(10014337466658779899)
XLA Ops:
  0.0 12.9 %shard_map.64 = f32[8,1024]{1,0:T(8,128)S(1)} custom-call(s32[8]{0:T(128)} %lengths.1, bf16[8,1,4,128]{3,2,1,0:T(4,128)(2,1)} %queries.1, bf16[8,1,256,128]{3,2,1,0:T(8,128)(2,1)} %keys.1, bf16[8,1,256,128]{3,2,1,0:T(8,128)(2,1)} %values.1, bf16[1,1,128,8192]{3,2,1,0:T(8,128)(2,1)} %weights.1, f32[8,1024]{1,0:T(8,128)} %residual.1), custom_call_target="tpu_custom_call" | custom-call | flops 16777216 | bytes 2097152 | tf_op jit(solution)/shard_map/pallas_call | solution.py:247
  12.9 0.6 %copy.8 = f32[8,1024]{1,0:T(8,128)} copy(f32[8,1024]{1,0:T(8,128)S(1)} %shard_map.64) | data formatting | bytes 65536

commit v4 on v3

--- a/solution.py
+++ b/solution.py
@@ -9,7 +9,7 @@
 from jax.sharding import PartitionSpec as P
 
 BLOCK_POSITIONS = 32
-DIRECT_COLUMNS = 256
+DIRECT_COLUMNS = 0
 MESH = pl.DeviceIdType.MESH
 
 
@@ -38,25 +38,16 @@
     share = out.shape[1]
     blocks = n_seq * n_kvh
 
-    step = rows // 4
     loads = {
-        "lengths": pltpu.make_async_copy(lengths, l_buf, load_sem.at[0]),
+        "keys": pltpu.make_async_copy(keys, k_buf, load_sem.at[0]),
         "queries": pltpu.make_async_copy(queries, q_buf, load_sem.at[1]),
+        "lengths": pltpu.make_async_copy(lengths, l_buf, load_sem.at[2]),
+        "values": pltpu.make_async_copy(values, v_buf, load_sem.at[3]),
+        "weights": pltpu.make_async_copy(weights.at[0, 0], w_buf, load_sem.at[4]),
+        "residual": pltpu.make_async_copy(residual, r_buf, load_sem.at[5]),
     }
-    for n in range(4):
-        some = pl.ds(n * step, step)
-        loads["keys", n * step] = pltpu.make_async_copy(
-            keys.at[some], k_buf.at[some], load_sem.at[2 + n]
-        )
-    for n in range(4):
-        some = pl.ds(n * step, step)
-        loads["values", n * step] = pltpu.make_async_copy(
-            values.at[some], v_buf.at[some], load_sem.at[6 + n]
-        )
-    loads["weights"] = pltpu.make_async_copy(weights.at[0, 0], w_buf, load_sem.at[10])
-    loads["residual"] = pltpu.make_async_copy(residual, r_buf, load_sem.at[11])
-    for load in loads.values():
-        load.start()
+    for name in ("keys", "queries", "lengths", "values"):
+        loads[name].start()
 
     seq_peers = [partner(seq, i, n_seq) for i in range(n_seq)]
     kvh_peers = [partner(kvh, j, n_kvh) for j in range(n_kvh)]
@@ -86,10 +77,11 @@
         [q_rows[pl.ds(g, rows, stride=heads), :] for g in range(heads)], axis=0
     ).astype(jnp.bfloat16)
 
+    loads["keys"].wait()
+    loads["weights"].start()
+    loads["residual"].start()
     scores = jnp.zeros((heads, rows, slots), jnp.float32)
     for b in range(rows):
-        if b % step == 0:
-            loads["keys", b].wait()
         full = lax.dot_general(
             q, k_buf[b, 0], (((1,), (1,)), ((), ())), preferred_element_type=jnp.float32
         ).reshape(heads, rows, slots)
@@ -99,10 +91,9 @@
     probs = jnp.exp(scores - top)
     total = jnp.sum(probs, axis=2, keepdims=True)
     probs = probs.reshape(heads * rows, slots).astype(jnp.bfloat16)
+    loads["values"].wait()
     summed = jnp.zeros((heads, rows, size), jnp.float32)
     for b in range(rows):
-        if b % step == 0:
-            loads["values", b].wait()
         full = jnp.dot(probs, v_buf[b, 0], preferred_element_type=jnp.float32)
         summed = jnp.where((out_row == b)[None], full.reshape(heads, rows, size), summed)
     part_send[:, :rows, :] = summed / total
@@ -266,7 +257,7 @@
             pltpu.VMEM((n_seq, rows, share), f32),
             pltpu.VMEM((n_seq, rows, share), f32),
             pltpu.VMEM((n_seq * n_kvh if share % 128 else 1, rows, share), f32),
-            dma((12,)),
+            dma((6,)),
             dma((n_seq,)),
             dma((n_seq,)),
             dma((n_seq, n_kvh)),

time: 13.7 us -> 12.9 us (0.942)
  Pallas kernels: 12.9 us -> 12.1 us
    pallas_call x1, Pallas kernels: 12.9 us -> 12.1 us  [body(): pl.pallas_call(functools.partial(kernel, n_seq, n_kvh, cut), out_shape=ja...]
where the time goes in v4:
time: 12.9 us; the launch traced here: 12.8 us
  Pallas kernels  12.1 us (94%)
  local copies, waits for them, and re-layouts  0.62 us (5%)
    pallas_call x1, Pallas kernels, body(): pl.pallas_call(functools.partial(kernel, n_seq, n_kvh, cut), out_shape=ja...  12.1 us
    unnamed x1, local copies, waits for them, and re-layouts  0.62 us

profile of v4, /device:TPU:0, one launch (start us, length us, event | category | flops | bytes accessed | tf_op | source)
XLA Modules:
  0.0 12.8 jit_solution(6979643788489684965)
XLA Ops:
  0.0 12.1 %shard_map.64 = f32[8,1024]{1,0:T(8,128)S(1)} custom-call(s32[8]{0:T(128)} %lengths.1, bf16[8,1,4,128]{3,2,1,0:T(4,128)(2,1)} %queries.1, bf16[8,1,256,128]{3,2,1,0:T(8,128)(2,1)} %keys.1, bf16[8,1,256,128]{3,2,1,0:T(8,128)(2,1)} %values.1, bf16[1,1,128,8192]{3,2,1,0:T(8,128)(2,1)} %weights.1, f32[8,1024]{1,0:T(8,128)} %residual.1), custom_call_target="tpu_custom_call" | custom-call | flops 16777216 | bytes 2097152 | tf_op jit(solution)/shard_map/pallas_call | solution.py:238
  12.2 0.6 %copy.8 = f32[8,1024]{1,0:T(8,128)} copy(f32[8,1024]{1,0:T(8,128)S(1)} %shard_map.64) | data formatting | bytes 65536

commit v5 on v4

--- a/solution.py
+++ b/solution.py
@@ -9,7 +9,7 @@
 from jax.sharding import PartitionSpec as P
 
 BLOCK_POSITIONS = 32
-DIRECT_COLUMNS = 0
+DIRECT_COLUMNS = 1024
 MESH = pl.DeviceIdType.MESH
 
 

time: 12.9 us -> 11.9 us (0.922)
  Pallas kernels: 12.1 us -> 11.1 us
    pallas_call x1, Pallas kernels: 12.1 us -> 11.1 us  [body(): pl.pallas_call(functools.partial(kernel, n_seq, n_kvh, cut), out_shape=ja...]
where the time goes in v5:
time: 11.9 us; the launch traced here: 11.7 us
  Pallas kernels  11.1 us (93%)
  local copies, waits for them, and re-layouts  0.62 us (5%)
    pallas_call x1, Pallas kernels, body(): pl.pallas_call(functools.partial(kernel, n_seq, n_kvh, cut), out_shape=ja...  11.1 us
    unnamed x1, local copies, waits for them, and re-layouts  0.62 us

profile of v5, /device:TPU:0, one launch (start us, length us, event | category | flops | bytes accessed | tf_op | source)
XLA Modules:
  0.0 11.7 jit_solution(188807850181731198)
XLA Ops:
  0.0 11.1 %shard_map.64 = f32[8,1024]{1,0:T(8,128)S(1)} custom-call(s32[8]{0:T(128)} %lengths.1, bf16[8,1,4,128]{3,2,1,0:T(4,128)(2,1)} %queries.1, bf16[8,1,256,128]{3,2,1,0:T(8,128)(2,1)} %keys.1, bf16[8,1,256,128]{3,2,1,0:T(8,128)(2,1)} %values.1, bf16[1,1,128,8192]{3,2,1,0:T(8,128)(2,1)} %weights.1, f32[8,1024]{1,0:T(8,128)} %residual.1), custom_call_target="tpu_custom_call" | custom-call | flops 16777216 | bytes 2097152 | tf_op jit(solution)/shard_map/pallas_call | solution.py:238
  11.1 0.6 %copy.8 = f32[8,1024]{1,0:T(8,128)} copy(f32[8,1024]{1,0:T(8,128)S(1)} %shard_map.64) | data formatting | bytes 65536

commit v6 on v5

--- a/solution.py
+++ b/solution.py
@@ -46,8 +46,8 @@
         "weights": pltpu.make_async_copy(weights.at[0, 0], w_buf, load_sem.at[4]),
         "residual": pltpu.make_async_copy(residual, r_buf, load_sem.at[5]),
     }
-    for name in ("keys", "queries", "lengths", "values"):
-        loads[name].start()
+    for load in loads.values():
+        load.start()
 
     seq_peers = [partner(seq, i, n_seq) for i in range(n_seq)]
     kvh_peers = [partner(kvh, j, n_kvh) for j in range(n_kvh)]
@@ -78,8 +78,6 @@
     ).astype(jnp.bfloat16)
 
     loads["keys"].wait()
-    loads["weights"].start()
-    loads["residual"].start()
     scores = jnp.zeros((heads, rows, slots), jnp.float32)
     for b in range(rows):
         full = lax.dot_general(
@@ -148,7 +146,7 @@
     direct_copies = {}
     core_copies = {}
     for i in order:
-        for j in range(n_kvh):
+        for j in reversed(range(n_kvh)):
             if i and cut:
                 direct_send[i, j] = contribution(i, j, 0, cut)
                 target = {"seq": seq_peers[i]}
@@ -205,20 +203,30 @@
             seq_copies[i] = copy
             sends.append(copy)
     result = r_buf[...] + contribution(0, 0, 0, share)
-    for j in range(1, n_kvh):
-        core_copies[0, j].wait_recv()
-        result = result + core_recv[0, j]
-    out[...] = result
-    if cut:
-        result = out[:, low]
-        for i in order[:-1][::-1]:
-            for j in range(n_kvh):
-                direct_copies[i, j].wait_recv()
-                result = result + direct_recv[i, j]
-        out[:, low] = result
-    if cut < share:
+    if cut == share:
+        for i in order[:-2] + [0] + order[-2:-1]:
+            for j in reversed(range(n_kvh)):
+                if i:
+                    direct_copies[i, j].wait_recv()
+                    result = result + direct_recv[i, j]
+                elif j:
+                    core_copies[i, j].wait_recv()
+                    result = result + core_recv[i, j]
+        out[...] = result
+    else:
+        for j in range(1, n_kvh):
+            core_copies[0, j].wait_recv()
+            result = result + core_recv[0, j]
+        out[...] = result
+        if cut:
+            result = out[:, low]
+            for i in order[:-1]:
+                for j in range(n_kvh):
+                    direct_copies[i, j].wait_recv()
+                    result = result + direct_recv[i, j]
+            out[:, low] = result
         result = out[:, high]
-        for i in order[:-1][::-1]:
+        for i in order[:-1]:
             seq_copies[i].wait_recv()
             result = result + seq_recv[i, :, high]
         out[:, high] = result

time: 11.9 us -> 12.5 us (1.050)
  Pallas kernels: 11.1 us -> 11.8 us
    pallas_call x1, Pallas kernels: 11.1 us -> 11.8 us  [body(): pl.pallas_call(functools.partial(kernel, n_seq, n_kvh, cut), out_shape=ja...]
where the time goes in v6:
time: 12.5 us; the launch traced here: 12.4 us
  Pallas kernels  11.8 us (94%)
  local copies, waits for them, and re-layouts  0.62 us (5%)
    pallas_call x1, Pallas kernels, body(): pl.pallas_call(functools.partial(kernel, n_seq, n_kvh, cut), out_shape=ja...  11.8 us
    unnamed x1, local copies, waits for them, and re-layouts  0.62 us

profile of v6, /device:TPU:0, one launch (start us, length us, event | category | flops | bytes accessed | tf_op | source)
XLA Modules:
  0.0 12.4 jit_solution(6750578206152155260)
XLA Ops:
  0.0 11.8 %shard_map.64 = f32[8,1024]{1,0:T(8,128)S(1)} custom-call(s32[8]{0:T(128)} %lengths.1, bf16[8,1,4,128]{3,2,1,0:T(4,128)(2,1)} %queries.1, bf16[8,1,256,128]{3,2,1,0:T(8,128)(2,1)} %keys.1, bf16[8,1,256,128]{3,2,1,0:T(8,128)(2,1)} %values.1, bf16[1,1,128,8192]{3,2,1,0:T(8,128)(2,1)} %weights.1, f32[8,1024]{1,0:T(8,128)} %residual.1), custom_call_target="tpu_custom_call" | custom-call | flops 16777216 | bytes 2097152 | tf_op jit(solution)/shard_map/pallas_call | solution.py:246
  11.8 0.6 %copy.8 = f32[8,1024]{1,0:T(8,128)} copy(f32[8,1024]{1,0:T(8,128)S(1)} %shard_map.64) | data formatting | bytes 65536

commit v7 on v6

--- a/solution.py
+++ b/solution.py
@@ -46,8 +46,8 @@
         "weights": pltpu.make_async_copy(weights.at[0, 0], w_buf, load_sem.at[4]),
         "residual": pltpu.make_async_copy(residual, r_buf, load_sem.at[5]),
     }
-    for load in loads.values():
-        load.start()
+    for name in ("keys", "queries", "lengths", "values"):
+        loads[name].start()
 
     seq_peers = [partner(seq, i, n_seq) for i in range(n_seq)]
     kvh_peers = [partner(kvh, j, n_kvh) for j in range(n_kvh)]
@@ -78,6 +78,8 @@
     ).astype(jnp.bfloat16)
 
     loads["keys"].wait()
+    loads["weights"].start()
+    loads["residual"].start()
     scores = jnp.zeros((heads, rows, slots), jnp.float32)
     for b in range(rows):
         full = lax.dot_general(
@@ -146,7 +148,7 @@
     direct_copies = {}
     core_copies = {}
     for i in order:
-        for j in reversed(range(n_kvh)):
+        for j in range(n_kvh):
             if i and cut:
                 direct_send[i, j] = contribution(i, j, 0, cut)
                 target = {"seq": seq_peers[i]}
@@ -205,7 +207,7 @@
     result = r_buf[...] + contribution(0, 0, 0, share)
     if cut == share:
         for i in order[:-2] + [0] + order[-2:-1]:
-            for j in reversed(range(n_kvh)):
+            for j in range(n_kvh):
                 if i:
                     direct_copies[i, j].wait_recv()
                     result = result + direct_recv[i, j]

time: 12.5 us -> 11.9 us (0.952)
  Pallas kernels: 11.8 us -> 11.1 us
    pallas_call x1, Pallas kernels: 11.8 us -> 11.1 us  [body(): pl.pallas_call(functools.partial(kernel, n_seq, n_kvh, cut), out_shape=ja...]
where the time goes in v7:
time: 11.9 us; the launch traced here: 11.7 us
  Pallas kernels  11.1 us (93%)
  local copies, waits for them, and re-layouts  0.62 us (5%)
    pallas_call x1, Pallas kernels, body(): pl.pallas_call(functools.partial(kernel, n_seq, n_kvh, cut), out_shape=ja...  11.1 us
    unnamed x1, local copies, waits for them, and re-layouts  0.62 us

profile of v7, /device:TPU:0, one launch (start us, length us, event | category | flops | bytes accessed | tf_op | source)
XLA Modules:
  0.0 11.7 jit_solution(8222352734862145611)
XLA Ops:
  0.0 11.1 %shard_map.64 = f32[8,1024]{1,0:T(8,128)S(1)} custom-call(s32[8]{0:T(128)} %lengths.1, bf16[8,1,4,128]{3,2,1,0:T(4,128)(2,1)} %queries.1, bf16[8,1,256,128]{3,2,1,0:T(8,128)(2,1)} %keys.1, bf16[8,1,256,128]{3,2,1,0:T(8,128)(2,1)} %values.1, bf16[1,1,128,8192]{3,2,1,0:T(8,128)(2,1)} %weights.1, f32[8,1024]{1,0:T(8,128)} %residual.1), custom_call_target="tpu_custom_call" | custom-call | flops 16777216 | bytes 2097152 | tf_op jit(solution)/shard_map/pallas_call | solution.py:248
  11.1 0.6 %copy.8 = f32[8,1024]{1,0:T(8,128)} copy(f32[8,1024]{1,0:T(8,128)S(1)} %shard_map.64) | data formatting | bytes 65536

commit v8 on v7

--- a/solution.py
+++ b/solution.py
@@ -147,9 +147,9 @@
     low, high = pl.ds(0, cut), pl.ds(cut, share - cut)
     direct_copies = {}
     core_copies = {}
-    for i in order:
+    if cut:
         for j in range(n_kvh):
-            if i and cut:
+            for i in order[:-1]:
                 direct_send[i, j] = contribution(i, j, 0, cut)
                 target = {"seq": seq_peers[i]}
                 if j:
@@ -165,6 +165,7 @@
                 copy.start()
                 direct_copies[i, j] = copy
                 sends.append(copy)
+    for i in order:
         for j in range(1, n_kvh):
             first = cut if i else 0
             if first < share:
@@ -206,14 +207,13 @@
             sends.append(copy)
     result = r_buf[...] + contribution(0, 0, 0, share)
     if cut == share:
-        for i in order[:-2] + [0] + order[-2:-1]:
-            for j in range(n_kvh):
-                if i:
-                    direct_copies[i, j].wait_recv()
-                    result = result + direct_recv[i, j]
-                elif j:
-                    core_copies[i, j].wait_recv()
-                    result = result + core_recv[i, j]
+        for j in range(n_kvh):
+            for i in order[:-1]:
+                direct_copies[i, j].wait_recv()
+                result = result + direct_recv[i, j]
+        for j in range(1, n_kvh):
+            core_copies[0, j].wait_recv()
+            result = result + core_recv[0, j]
         out[...] = result
     else:
         for j in range(1, n_kvh):

time: 11.9 us -> 11.8 us (level)
  no operation moved by 1% of the time
where the time goes in v8:
time: 11.8 us; the launch traced here: 11.7 us
  Pallas kernels  11 us (93%)
  local copies, waits for them, and re-layouts  0.62 us (5%)
    pallas_call x1, Pallas kernels, body(): pl.pallas_call(functools.partial(kernel, n_seq, n_kvh, cut), out_shape=ja...  11 us
    unnamed x1, local copies, waits for them, and re-layouts  0.62 us

profile of v8, /device:TPU:0, one launch (start us, length us, event | category | flops | bytes accessed | tf_op | source)
XLA Modules:
  0.0 11.7 jit_solution(14717933475923188817)
XLA Ops:
  0.0 11.0 %shard_map.64 = f32[8,1024]{1,0:T(8,128)S(1)} custom-call(s32[8]{0:T(128)} %lengths.1, bf16[8,1,4,128]{3,2,1,0:T(4,128)(2,1)} %queries.1, bf16[8,1,256,128]{3,2,1,0:T(8,128)(2,1)} %keys.1, bf16[8,1,256,128]{3,2,1,0:T(8,128)(2,1)} %values.1, bf16[1,1,128,8192]{3,2,1,0:T(8,128)(2,1)} %weights.1, f32[8,1024]{1,0:T(8,128)} %residual.1), custom_call_target="tpu_custom_call" | custom-call | flops 16777216 | bytes 2097152 | tf_op jit(solution)/shard_map/pallas_call | solution.py:248
  11.1 0.6 %copy.8 = f32[8,1024]{1,0:T(8,128)} copy(f32[8,1024]{1,0:T(8,128)S(1)} %shard_map.64) | data formatting | bytes 65536

commit v9 on v8

--- a/solution.py
+++ b/solution.py
@@ -38,16 +38,24 @@
     share = out.shape[1]
     blocks = n_seq * n_kvh
 
-    loads = {
-        "keys": pltpu.make_async_copy(keys, k_buf, load_sem.at[0]),
-        "queries": pltpu.make_async_copy(queries, q_buf, load_sem.at[1]),
-        "lengths": pltpu.make_async_copy(lengths, l_buf, load_sem.at[2]),
-        "values": pltpu.make_async_copy(values, v_buf, load_sem.at[3]),
-        "weights": pltpu.make_async_copy(weights.at[0, 0], w_buf, load_sem.at[4]),
-        "residual": pltpu.make_async_copy(residual, r_buf, load_sem.at[5]),
-    }
-    for name in ("keys", "queries", "lengths", "values"):
-        loads[name].start()
+    pieces = 4 if rows % 4 == 0 else 1
+    step = rows // pieces
+    loads = {}
+    for n in range(pieces):
+        some = pl.ds(n * step, step)
+        loads["keys", n * step] = pltpu.make_async_copy(
+            keys.at[some], k_buf.at[some], load_sem.at[5 + n]
+        )
+        loads["keys", n * step].start()
+        if n == 0:
+            loads["queries"] = pltpu.make_async_copy(queries, q_buf, load_sem.at[0])
+            loads["queries"].start()
+    loads["lengths"] = pltpu.make_async_copy(lengths, l_buf, load_sem.at[1])
+    loads["values"] = pltpu.make_async_copy(values, v_buf, load_sem.at[2])
+    loads["lengths"].start()
+    loads["values"].start()
+    loads["weights"] = pltpu.make_async_copy(weights.at[0, 0], w_buf, load_sem.at[3])
+    loads["residual"] = pltpu.make_async_copy(residual, r_buf, load_sem.at[4])
 
     seq_peers = [partner(seq, i, n_seq) for i in range(n_seq)]
     kvh_peers = [partner(kvh, j, n_kvh) for j in range(n_kvh)]
@@ -77,15 +85,16 @@
         [q_rows[pl.ds(g, rows, stride=heads), :] for g in range(heads)], axis=0
     ).astype(jnp.bfloat16)
 
-    loads["keys"].wait()
-    loads["weights"].start()
-    loads["residual"].start()
     scores = jnp.zeros((heads, rows, slots), jnp.float32)
     for b in range(rows):
+        if b % step == 0:
+            loads["keys", b].wait()
         full = lax.dot_general(
             q, k_buf[b, 0], (((1,), (1,)), ((), ())), preferred_element_type=jnp.float32
         ).reshape(heads, rows, slots)
         scores = jnp.where((row == b)[None], full, scores)
+    loads["weights"].start()
+    loads["residual"].start()
     scores = jnp.where(live[None], scores * (1.0 / math.sqrt(size)), -1e30)
     top = jnp.max(scores, axis=2, keepdims=True)
     probs = jnp.exp(scores - top)
@@ -267,7 +276,7 @@
             pltpu.VMEM((n_seq, rows, share), f32),
             pltpu.VMEM((n_seq, rows, share), f32),
             pltpu.VMEM((n_seq * n_kvh if share % 128 else 1, rows, share), f32),
-            dma((6,)),
+            dma((9,)),
             dma((n_seq,)),
             dma((n_seq,)),
             dma((n_seq, n_kvh)),

time: 11.8 us -> 12 us (1.017)
  Pallas kernels: 11 us -> 11.2 us
where the time goes in v9:
time: 12 us; the launch traced here: 11.8 us
  Pallas kernels  11.2 us (93%)
  local copies, waits for them, and re-layouts  0.62 us (5%)
    pallas_call x1, Pallas kernels, body(): pl.pallas_call(functools.partial(kernel, n_seq, n_kvh, cut), out_shape=ja...  11.2 us
    unnamed x1, local copies, waits for them, and re-layouts  0.62 us

profile of v9, /device:TPU:0, one launch (start us, length us, event | category | flops | bytes accessed | tf_op | source)
XLA Modules:
  0.0 11.8 jit_solution(14315407148199893774)
XLA Ops:
  0.0 11.2 %shard_map.64 = f32[8,1024]{1,0:T(8,128)S(1)} custom-call(s32[8]{0:T(128)} %lengths.1, bf16[8,1,4,128]{3,2,1,0:T(4,128)(2,1)} %queries.1, bf16[8,1,256,128]{3,2,1,0:T(8,128)(2,1)} %keys.1, bf16[8,1,256,128]{3,2,1,0:T(8,128)(2,1)} %values.1, bf16[1,1,128,8192]{3,2,1,0:T(8,128)(2,1)} %weights.1, f32[8,1024]{1,0:T(8,128)} %residual.1), custom_call_target="tpu_custom_call" | custom-call | flops 16777216 | bytes 2097152 | tf_op jit(solution)/shard_map/pallas_call | solution.py:257
  11.2 0.6 %copy.8 = f32[8,1024]{1,0:T(8,128)} copy(f32[8,1024]{1,0:T(8,128)S(1)} %shard_map.64) | data formatting | bytes 65536

commit v10 on v2

v10 whole, which is shorter than its diff:
```python
import functools
import math

import jax
import jax.numpy as jnp
from jax import lax
from jax.experimental import pallas as pl
from jax.experimental.pallas import tpu as pltpu
from jax.sharding import PartitionSpec as P

BLOCK_POSITIONS = 32
MESH = pl.DeviceIdType.MESH


def partner(me, step, count):
    result = 0
    bit = 1
    while bit < count:
        own = lax.rem(lax.div(me, bit), 2)
        result = result + bit * (1 - own if (step // bit) % 2 else own)
        bit *= 2
    return result


def kernel(
    n_seq, n_kvh,
    lengths, queries, keys, values, weights, residual, out,
    l_buf, q_buf, q_rows, k_buf, v_buf, w_buf, r_buf,
    part_send, part_recv, direct_send, direct_recv, contrib,
    load_sem, ps_sem, pr_sem, ds_sem, dr_sem,
):
    seq = lax.axis_index("seq")
    kvh = lax.axis_index("kvh")
    rows, _, heads, size = queries.shape
    slots = keys.shape[2]
    share = out.shape[1]
    blocks = n_seq * n_kvh

    loads = {
        "keys": pltpu.make_async_copy(keys, k_buf, load_sem.at[0]),
        "queries": pltpu.make_async_copy(queries, q_buf, load_sem.at[1]),
        "lengths": pltpu.make_async_copy(lengths, l_buf, load_sem.at[2]),
        "values": pltpu.make_async_copy(values, v_buf, load_sem.at[3]),
        "weights": pltpu.make_async_copy(weights.at[0, 0], w_buf, load_sem.at[4]),
        "residual": pltpu.make_async_copy(residual, r_buf, load_sem.at[5]),
    }
    for name in ("keys", "queries", "lengths", "values"):
        loads[name].start()

    seq_peers = [partner(seq, i, n_seq) for i in range(n_seq)]
    kvh_peers = [partner(kvh, j, n_kvh) for j in range(n_kvh)]
    barrier = pltpu.get_barrier_semaphore()
    greeted = 0
    for i in range(n_seq):
        for j in range(n_kvh):
            if i or j:
                target = {"seq": seq_peers[i], "kvh": kvh_peers[j]}
                pl.semaphore_signal(barrier, inc=1, device_id=target, device_id_type=MESH)
                greeted += 1

    row = lax.broadcasted_iota(jnp.int32, (rows, slots), 0)
    slot = lax.broadcasted_iota(jnp.int32, (rows, slots), 1)
    length = jnp.zeros((rows, slots), jnp.int32)
    loads["lengths"].wait()
    for b in range(rows):
        length = jnp.where(row == b, l_buf[b], length)
    position = (slot // BLOCK_POSITIONS * n_seq + seq) * BLOCK_POSITIONS + slot % BLOCK_POSITIONS
    live = position < length
    out_row = lax.broadcasted_iota(jnp.int32, (rows, size), 0)

    loads["queries"].wait()
    for b in range(rows):
        q_rows[pl.ds(b * heads, heads), :] = q_buf[b, 0].astype(jnp.float32)
    q = jnp.concatenate(
        [q_rows[pl.ds(g, rows, stride=heads), :] for g in range(heads)], axis=0
    ).astype(jnp.bfloat16)

    loads["keys"].wait()
    loads["weights"].start()
    loads["residual"].start()
    scores = jnp.zeros((heads, rows, slots), jnp.float32)
    for b in range(rows):
        full = lax.dot_general(
            q, k_buf[b, 0], (((1,), (1,)), ((), ())), preferred_element_type=jnp.float32
        ).reshape(heads, rows, slots)
        scores = jnp.where((row == b)[None], full, scores)
    scores = jnp.where(live[None], scores * (1.0 / math.sqrt(size)), -1e30)
    top = jnp.max(scores, axis=2, keepdims=True)
    probs = jnp.exp(scores - top)
    total = jnp.sum(probs, axis=2, keepdims=True)
    probs = probs.reshape(heads * rows, slots).astype(jnp.bfloat16)
    loads["values"].wait()
    summed = jnp.zeros((heads, rows, size), jnp.float32)
    for b in range(rows):
        full = jnp.dot(probs, v_buf[b, 0], preferred_element_type=jnp.float32)
        summed = jnp.where((out_row == b)[None], full.reshape(heads, rows, size), summed)
    part_send[:, :rows, :] = summed / total
    part_send[:, rows:, :] = jnp.broadcast_to(top + jnp.log(total), (heads, rows, size))

    pl.semaphore_wait(barrier, greeted)
    order = list(range(n_seq - 1, 0, -1))
    for i in order:
        pltpu.make_async_remote_copy(
            src_ref=part_send.at[seq_peers[i]],
            dst_ref=part_recv.at[i - 1],
            send_sem=ps_sem,
            recv_sem=pr_sem,
            device_id={"seq": seq_peers[i]},
            device_id_type=MESH,
        ).start()

    loads["weights"].wait()
    loads["residual"].wait()
    pltpu.make_async_copy(part_recv, part_recv, pr_sem).wait()
    parts = [part_send[seq]] + [part_recv[i] for i in range(n_seq - 1)]
    highest = functools.reduce(jnp.maximum, [part[rows:] for part in parts])
    factors = [jnp.exp(part[rows:] - highest) for part in parts]
    joined = sum(factor * part[:rows] for factor, part in zip(factors, parts))
    attended = (joined / sum(factors)).astype(jnp.bfloat16)

    aligned = share % 128 == 0
    if not aligned:
        for first in range(0, blocks * share, 1024):
            tile = jnp.dot(
                attended, w_buf[:, first:first + 1024], preferred_element_type=jnp.float32
            )
            for block in range(1024 // share):
                contrib[first // share + block] = tile[:, block * share:(block + 1) * share]

    def contribution(block):
        if not aligned:
            return contrib[block]
        columns = pl.ds(pl.multiple_of(block * share, 128), share)
        return jnp.dot(attended, w_buf[:, columns], preferred_element_type=jnp.float32)

    pairs = [(i, j) for j in range(n_kvh) for i in order] + [(0, j) for j in range(1, n_kvh)]
    for i, j in pairs:
        slot = i * n_kvh + j - 1
        direct_send[slot] = contribution(seq_peers[i] * n_kvh + kvh_peers[j])
        target = {"seq": seq_peers[i], "kvh": kvh_peers[j]}
        pltpu.make_async_remote_copy(
            src_ref=direct_send.at[slot],
            dst_ref=direct_recv.at[slot],
            send_sem=ds_sem,
            recv_sem=dr_sem,
            device_id=target,
            device_id_type=MESH,
        ).start()
    result = r_buf[...] + contribution(seq * n_kvh + kvh)
    pltpu.make_async_copy(part_recv, part_recv, ps_sem).wait()
    pltpu.make_async_copy(direct_recv, direct_recv, dr_sem).wait()
    for slot in range(blocks - 1):
        result = result + direct_recv[slot]
    out[...] = result
    pltpu.make_async_copy(direct_send, direct_send, ds_sem).wait()


def body(n_seq, n_kvh, queries, keys, values, lengths, weights, residual):
    rows, _, heads, size = queries.shape
    slots = keys.shape[2]
    features = weights.shape[3]
    share = residual.shape[1]
    f32, bf16 = jnp.float32, jnp.bfloat16
    dma = pltpu.SemaphoreType.DMA
    in_hbm = pl.BlockSpec(memory_space=pltpu.HBM)
    return pl.pallas_call(
        functools.partial(kernel, n_seq, n_kvh),
        out_shape=jax.ShapeDtypeStruct((rows, share), f32),
        in_specs=[in_hbm] * 6,
        out_specs=pl.BlockSpec(memory_space=pltpu.VMEM),
        scratch_shapes=[
            pltpu.SMEM((rows,), jnp.int32),
            pltpu.VMEM((rows, 1, heads, size), bf16),
            pltpu.VMEM((rows * heads, size), f32),
            pltpu.VMEM((rows, 1, slots, size), bf16),
            pltpu.VMEM((rows, 1, slots, size), bf16),
            pltpu.VMEM((size, features), bf16),
            pltpu.VMEM((rows, share), f32),
            pltpu.VMEM((heads, 2 * rows, size), f32),
            pltpu.VMEM((n_seq - 1, 2 * rows, size), f32),
            pltpu.VMEM((n_seq * n_kvh - 1, rows, share), f32),
            pltpu.VMEM((n_seq * n_kvh - 1, rows, share), f32),
            pltpu.VMEM((n_seq * n_kvh if share % 128 else 1, rows, share), f32),
            dma((6,)),
            dma,
            dma,
            dma,
            dma,
        ],
        compiler_params=pltpu.CompilerParams(
            collective_id=0, has_side_effects=True, vmem_limit_bytes=40 * 1024 * 1024
        ),
        cost_estimate=pl.CostEstimate(
            flops=2 * rows * size * features, bytes_accessed=2 * size * features, transcendentals=0
        ),
    )(*[
        pltpu.with_memory_space_constraint(array, pltpu.HBM)
        for array in (lengths, queries, keys, values, weights, residual)
    ])


def solution(mesh):
    in_specs = (
        P("rep", "kvh", None, None),
        P("rep", "kvh", "seq", None),
        P("rep", "kvh", "seq", None),
        P("rep"),
        P("kvh", "seq", None, None),
        P("rep", ("seq", "kvh")),
    )
    out_specs = P("rep", ("seq", "kvh"))
    run = functools.partial(body, mesh.shape["seq"], mesh.shape["kvh"])
    return jax.shard_map(run, mesh=mesh, in_specs=in_specs, out_specs=out_specs, check_vma=False)
```

time: 12.8 us -> 11.4 us (0.89)
  Pallas kernels: 12 us -> 10.6 us
    pallas_call x1, Pallas kernels: 12 us -> 10.6 us  [body(): pl.pallas_call(functools.partial(kernel, n_seq, n_kvh), out_shape=jax.Sha...]
where the time goes in v10:
time: 11.4 us; the launch traced here: 11.3 us
  Pallas kernels  10.6 us (93%)
  local copies, waits for them, and re-layouts  0.62 us (5%)
    pallas_call x1, Pallas kernels, body(): pl.pallas_call(functools.partial(kernel, n_seq, n_kvh), out_shape=jax.Sha...  10.6 us
    unnamed x1, local copies, waits for them, and re-layouts  0.62 us

profile of v10, /device:TPU:0, one launch (start us, length us, event | category | flops | bytes accessed | tf_op | source)
XLA Modules:
  0.0 11.3 jit_solution(6988814119864103402)
XLA Ops:
  0.0 10.6 %shard_map.64 = f32[8,1024]{1,0:T(8,128)S(1)} custom-call(s32[8]{0:T(128)} %lengths.1, bf16[8,1,4,128]{3,2,1,0:T(4,128)(2,1)} %queries.1, bf16[8,1,256,128]{3,2,1,0:T(8,128)(2,1)} %keys.1, bf16[8,1,256,128]{3,2,1,0:T(8,128)(2,1)} %values.1, bf16[1,1,128,8192]{3,2,1,0:T(8,128)(2,1)} %weights.1, f32[8,1024]{1,0:T(8,128)} %residual.1), custom_call_target="tpu_custom_call" | custom-call | flops 16777216 | bytes 2097152 | tf_op jit(solution)/shard_map/pallas_call | solution.py:166
  10.6 0.6 %copy.8 = f32[8,1024]{1,0:T(8,128)} copy(f32[8,1024]{1,0:T(8,128)S(1)} %shard_map.64) | data formatting | bytes 65536

commit v11 on v10

--- a/solution.py
+++ b/solution.py
@@ -134,18 +134,22 @@
         return jnp.dot(attended, w_buf[:, columns], preferred_element_type=jnp.float32)
 
     pairs = [(i, j) for j in range(n_kvh) for i in order] + [(0, j) for j in range(1, n_kvh)]
-    for i, j in pairs:
-        slot = i * n_kvh + j - 1
-        direct_send[slot] = contribution(seq_peers[i] * n_kvh + kvh_peers[j])
-        target = {"seq": seq_peers[i], "kvh": kvh_peers[j]}
-        pltpu.make_async_remote_copy(
-            src_ref=direct_send.at[slot],
-            dst_ref=direct_recv.at[slot],
-            send_sem=ds_sem,
-            recv_sem=dr_sem,
-            device_id=target,
-            device_id_type=MESH,
-        ).start()
+    done = 0
+    while done < len(pairs):
+        group = pairs[done:2 * done + 1]
+        done += len(group)
+        for i, j in group:
+            direct_send[i * n_kvh + j - 1] = contribution(seq_peers[i] * n_kvh + kvh_peers[j])
+        for i, j in group:
+            slot = i * n_kvh + j - 1
+            pltpu.make_async_remote_copy(
+                src_ref=direct_send.at[slot],
+                dst_ref=direct_recv.at[slot],
+                send_sem=ds_sem,
+                recv_sem=dr_sem,
+                device_id={"seq": seq_peers[i], "kvh": kvh_peers[j]},
+                device_id_type=MESH,
+            ).start()
     result = r_buf[...] + contribution(seq * n_kvh + kvh)
     pltpu.make_async_copy(part_recv, part_recv, ps_sem).wait()
     pltpu.make_async_copy(direct_recv, direct_recv, dr_sem).wait()

time: 11.4 us -> 11.4 us (level)
  no operation moved by 1% of the time
where the time goes in v11:
time: 11.4 us; the launch traced here: 11.3 us
  Pallas kernels  10.6 us (93%)
  local copies, waits for them, and re-layouts  0.62 us (5%)
    pallas_call x1, Pallas kernels, body(): pl.pallas_call(functools.partial(kernel, n_seq, n_kvh), out_shape=jax.Sha...  10.6 us
    unnamed x1, local copies, waits for them, and re-layouts  0.62 us

profile of v11, /device:TPU:0, one launch (start us, length us, event | category | flops | bytes accessed | tf_op | source)
XLA Modules:
  0.0 11.3 jit_solution(2438813415121647209)
XLA Ops:
  0.0 10.6 %shard_map.64 = f32[8,1024]{1,0:T(8,128)S(1)} custom-call(s32[8]{0:T(128)} %lengths.1, bf16[8,1,4,128]{3,2,1,0:T(4,128)(2,1)} %queries.1, bf16[8,1,256,128]{3,2,1,0:T(8,128)(2,1)} %keys.1, bf16[8,1,256,128]{3,2,1,0:T(8,128)(2,1)} %values.1, bf16[1,1,128,8192]{3,2,1,0:T(8,128)(2,1)} %weights.1, f32[8,1024]{1,0:T(8,128)} %residual.1), custom_call_target="tpu_custom_call" | custom-call | flops 16777216 | bytes 2097152 | tf_op jit(solution)/shard_map/pallas_call | solution.py:170
  10.6 0.6 %copy.8 = f32[8,1024]{1,0:T(8,128)} copy(f32[8,1024]{1,0:T(8,128)S(1)} %shard_map.64) | data formatting | bytes 65536

commit v12 on v11

--- a/solution.py
+++ b/solution.py
@@ -77,7 +77,6 @@
 
     loads["keys"].wait()
     loads["weights"].start()
-    loads["residual"].start()
     scores = jnp.zeros((heads, rows, slots), jnp.float32)
     for b in range(rows):
         full = lax.dot_general(
@@ -109,8 +108,8 @@
             device_id_type=MESH,
         ).start()
 
+    loads["residual"].start()
     loads["weights"].wait()
-    loads["residual"].wait()
     pltpu.make_async_copy(part_recv, part_recv, pr_sem).wait()
     parts = [part_send[seq]] + [part_recv[i] for i in range(n_seq - 1)]
     highest = functools.reduce(jnp.maximum, [part[rows:] for part in parts])
@@ -150,6 +149,7 @@
                 device_id={"seq": seq_peers[i], "kvh": kvh_peers[j]},
                 device_id_type=MESH,
             ).start()
+    loads["residual"].wait()
     result = r_buf[...] + contribution(seq * n_kvh + kvh)
     pltpu.make_async_copy(part_recv, part_recv, ps_sem).wait()
     pltpu.make_async_copy(direct_recv, direct_recv, dr_sem).wait()

time: 11.4 us -> 11.4 us (level)
  no operation moved by 1% of the time
where the time goes in v12:
time: 11.4 us; the launch traced here: 11.3 us
  Pallas kernels  10.6 us (93%)
  local copies, waits for them, and re-layouts  0.62 us (5%)
    pallas_call x1, Pallas kernels, body(): pl.pallas_call(functools.partial(kernel, n_seq, n_kvh), out_shape=jax.Sha...  10.6 us
    unnamed x1, local copies, waits for them, and re-layouts  0.62 us

profile of v12, /device:TPU:0, one launch (start us, length us, event | category | flops | bytes accessed | tf_op | source)
XLA Modules:
  0.0 11.3 jit_solution(16433102927836914650)
XLA Ops:
  0.0 10.6 %shard_map.64 = f32[8,1024]{1,0:T(8,128)S(1)} custom-call(s32[8]{0:T(128)} %lengths.1, bf16[8,1,4,128]{3,2,1,0:T(4,128)(2,1)} %queries.1, bf16[8,1,256,128]{3,2,1,0:T(8,128)(2,1)} %keys.1, bf16[8,1,256,128]{3,2,1,0:T(8,128)(2,1)} %values.1, bf16[1,1,128,8192]{3,2,1,0:T(8,128)(2,1)} %weights.1, f32[8,1024]{1,0:T(8,128)} %residual.1), custom_call_target="tpu_custom_call" | custom-call | flops 16777216 | bytes 2097152 | tf_op jit(solution)/shard_map/pallas_call | solution.py:170
  10.7 0.6 %copy.8 = f32[8,1024]{1,0:T(8,128)} copy(f32[8,1024]{1,0:T(8,128)S(1)} %shard_map.64) | data formatting | bytes 65536
